TPU v7x, 128 devices: a whole 4x4x4 slice. The times are simulated.
128 devices in a mesh: grp: 16 (over x, y), blk: 8 (over z, core).
Axes of the slice: x: 4, y: 4, z: 4, core: 2. Of those that a mesh axis runs over, the one named last changes fastest.
Arguments:
- embeddings: bfloat16 [65536, 768], P(('grp', 'blk'))
- assign: int32 [65536], P(('grp', 'blk')), may hold values from 0 to 127, as said below
- owner: int32 [128], replicated, may hold values from 0 to 15, as said below
- send_count: int32 [128, 16], P(('grp', 'blk')), may hold values from 0 to 64, as said below
- send_index: int32 [128, 16, 64], P(('grp', 'blk')), may hold values from 0 to 511, as said below
Outputs:
- max_sim: float32 [65536], P(('grp', 'blk'))
- centroid_cos: float32 [65536], P(('grp', 'blk'))
Inputs may be any that keep to these rules, and one draw needn't show every extreme that they name: `owner`: every group owns the same number of clusters. `assign`: every document's cluster is owned by the group in whose list of its device the document stands; a device may send many documents of one cluster. `send_count`: A device's counts sum to 512; a count may be anything from 0 to 64, and at least one group receives exactly 64 documents from every device. `send_index`: the used slots of a device's lists hold each of its documents exactly once; unused slots hold 0.
All inputs are finite; a program needn't handle non-finite values.
Results may differ from a plain program's by a relative error of at most 0.00085.
Values may be sent and summed in bfloat16 or wider, within the bound.
A program may use at most 64 MiB of HBM per device.

v0:
```python
import functools

import jax
import jax.numpy as jnp
from jax import lax
from jax.experimental import pallas as pl
from jax.experimental.pallas import tpu as pltpu
from jax.sharding import PartitionSpec as P

EPSILON = 1e-06
F32 = jnp.float32
BF16 = jnp.bfloat16

CHIPS = 64
ROWS = 512
WIDTH = 768
CLUSTERS = 128
GROUPS = 16
CAP = 64
BASE = 16
HALF = WIDTH // 2
LINES = 16
DEPTH = 4
POOL = 8
PARTS = ((0, 24, 256), (24, 32, 384), (56, 16, 128))
TOTAL = 72
HELD = 768
STARTS = (0, 256, 640)
LAST = len(PARTS) - 1
NONE = 1e30


def normalize(values):
    widened = values.astype(F32)
    return widened * lax.rsqrt(jnp.sum(widened * widened, axis=1, keepdims=True) + EPSILON)


def general(embeddings, assign, owner, send_count, send_index):
    rows_local = embeddings.shape[0]
    feature_width = embeddings.shape[1]
    groups = lax.axis_size("grp")
    clusters = owner.shape[0]
    capacity = send_index.shape[2]
    slot_total = groups * capacity
    unit_rows = normalize(embeddings)
    unit_low = unit_rows.astype(BF16)
    counts = send_count[0]
    listed = send_index[0]
    live_slot = jnp.arange(capacity, dtype=jnp.int32)[None, :] < counts[:, None]
    listed_cluster = assign[listed]
    owned_here = owner[listed_cluster] == jnp.arange(groups, dtype=jnp.int32)[:, None]
    kept_slot = live_slot & owned_here
    out_cluster = jnp.where(kept_slot, listed_cluster, -1)
    out_tag = jnp.where(kept_slot, lax.axis_index(("grp", "blk")) * rows_local + listed, -1)
    out_vector = unit_low[listed.reshape(-1)].reshape(groups, capacity, feature_width)
    got_vector, got_cluster, got_tag = (
        lax.all_to_all(out_vector, "grp", split_axis=0, concat_axis=0, tiled=True),
        lax.all_to_all(out_cluster, "grp", split_axis=0, concat_axis=0, tiled=True),
        lax.all_to_all(out_tag, "grp", split_axis=0, concat_axis=0, tiled=True),
    )
    own_vector = got_vector.reshape(slot_total, feature_width)
    own_cluster = got_cluster.reshape(slot_total)
    own_tag = got_tag.reshape(slot_total)

    def tile_best(current, shard_piece):
        other_vector, other_cluster, other_tag = shard_piece
        scores = jnp.einsum("id,jd->ij", own_vector, other_vector, preferred_element_type=F32)
        matched = (
            (own_cluster[:, None] == other_cluster[None, :])
            & (other_cluster[None, :] >= 0)
            & (own_tag[:, None] != other_tag[None, :])
        )
        return jnp.maximum(current, jnp.max(jnp.where(matched, scores, -1.0), axis=1))

    other_vector = lax.all_gather(own_vector, "blk", axis=0, tiled=True)
    other_cluster = lax.all_gather(own_cluster, "blk", axis=0, tiled=True)
    other_tag = lax.all_gather(own_tag, "blk", axis=0, tiled=True)
    length = other_vector.shape[0]
    number = length // slot_total
    stacked = (
        other_vector.reshape(number, slot_total, feature_width),
        other_cluster.reshape(number, slot_total),
        other_tag.reshape(number, slot_total),
    )

    def scan_step(carry, single):
        return (tile_best(carry, single), None)

    result, unused = lax.scan(scan_step, jnp.full((slot_total,), -1.0, F32), stacked)
    target = jnp.where(live_slot, listed, rows_local).reshape(-1)
    partial_sum = jax.ops.segment_sum(unit_rows, assign, num_segments=clusters)
    centre = normalize(lax.psum(partial_sum, ("grp", "blk")))
    nearness = jnp.sum(unit_low.astype(F32) * centre[assign], axis=1)
    returned = lax.all_to_all(
        result.reshape(groups, capacity), "grp", split_axis=0, concat_axis=0, tiled=True
    )
    has_entry = (
        jnp.zeros((rows_local,), jnp.int32)
        .at[target]
        .max(kept_slot.astype(jnp.int32).reshape(-1), mode="drop")
    )
    centroid_cos = jnp.where(has_entry > 0, nearness, 0.0)
    max_sim = jnp.full((rows_local,), -1.0, F32).at[target].max(returned.reshape(-1), mode="drop")
    return (max_sim, centroid_cos)


def iota(shape, axis):
    return lax.broadcasted_iota(jnp.int32, shape, axis)


def down(values):
    return jnp.sum(values, axis=0, keepdims=True)


def across(values):
    return jnp.sum(values, axis=1, keepdims=True)


def pick(mask, values):
    return jnp.where(mask, values, 0.0)


def as_column(row):
    size = row.shape[1]
    return across(pick(iota((size, size), 0) == iota((size, size), 1), row))


def as_row(column):
    size = column.shape[0]
    return down(pick(iota((size, size), 0) == iota((size, size), 1), column))


def dot(a, b):
    return jnp.dot(a, b, preferred_element_type=F32)


def dot_rows(a, b):
    return lax.dot_general(a, b, (((1,), (1,)), ((), ())), preferred_element_type=F32)


def onehot(mask):
    return jnp.where(mask, 1.0, 0.0).astype(BF16)


def thirds(values):
    first = values.astype(BF16).astype(F32)
    rest = values - first
    second = rest.astype(BF16).astype(F32)
    third = (rest - second).astype(BF16).astype(F32)
    return first, second, third


def rank_groups(count_ref):
    count_row = count_ref[...].astype(F32)
    count_column = as_column(count_row)
    sub, lane = iota((GROUPS, 128), 0), iota((GROUPS, 128), 1)
    count_lanes = down(pick(sub == lane, count_column))
    ahead = (count_column > count_lanes) | ((count_column == count_lanes) & (sub < lane))
    rank = down(jnp.where(ahead, 1.0, 0.0))
    return jnp.where(iota((1, 128), 1) < GROUPS, rank, 0.0), count_column


def place_documents(assign_ref, owner_ref, rank):
    owner_row = owner_ref[...].astype(F32)
    owner_column = as_column(owner_row)
    sub, lane = iota((CLUSTERS, CLUSTERS), 0), iota((CLUSTERS, CLUSTERS), 1)
    within = across(jnp.where((owner_column == owner_row) & (lane < sub), 1.0, 0.0))
    group_rank = across(pick(owner_column == lane.astype(F32), rank))
    place_column = group_rank * (CLUSTERS // GROUPS) + within
    member = iota((CLUSTERS, ROWS), 0) == assign_ref[...]
    place = down(pick(member, place_column))
    group = down(pick(member, owner_column))
    order = iota((CLUSTERS, ROWS), 0).astype(F32)
    at_place = order == place
    earlier = onehot(iota((ROWS, ROWS), 0) < iota((ROWS, ROWS), 1))
    before = dot(onehot(at_place), earlier)
    slot = down(pick(at_place, before))
    count_column = across(jnp.where(at_place, 1.0, 0.0))
    partner_count = down(pick(order == (CLUSTERS - 1) - place, count_column))
    slot = slot + jnp.where(place >= CHIPS, partner_count, 0.0)
    chip = jnp.minimum(place, (CLUSTERS - 1) - place)
    return group, chip.astype(jnp.int32), slot.astype(jnp.int32), as_row(count_column)


def missing_documents(index_ref, count_column, group):
    listed = index_ref[...]
    live = iota((GROUPS, CAP), 1).astype(F32) < count_column
    eye = onehot(iota((CAP, CAP), 0) == iota((CAP, CAP), 1))
    high = dot_rows(eye, jnp.where(live, listed >> 4, 0).astype(F32).astype(BF16))
    low = dot_rows(eye, jnp.where(live, listed & 15, 0).astype(F32).astype(BF16))
    alive = dot_rows(eye, onehot(live))
    slots = jnp.where(alive > 0.5, high * 16.0 + low, -1.0)
    document = iota((1, ROWS), 1).astype(F32)
    lane = iota((CAP, GROUPS), 1)

    def count(g, hits):
        column = across(pick(lane == g, slots))
        wanted = jnp.where(group == g.astype(F32), document, -2.0)
        return hits + jnp.where(column == wanted, 1.0, 0.0)

    hits = lax.fori_loop(0, GROUPS, count, jnp.zeros((CAP, ROWS), F32))
    return across(jnp.where(down(hits) > 0.5, 0.0, 1.0))


def send_order():
    order = []
    for step in range(CHIPS):
        high, middle, low = step // 16, (step // 4) % 4, step % 4
        order.append((low, (middle + low) % 4, (high + middle + low) % 4))
    near = [shift for shift in order if sum(min(d, 4 - d) for d in shift) <= 1] + [(2, 0, 0)]
    near.sort(key=lambda shift: -sum(min(d, 4 - d) for d in shift))
    return [shift for shift in order if shift not in near] + near


ORDER = send_order()
SELF = CHIPS - 1


def step_to(dx, dy, dz):
    shift = (dx & 3) * 16 + (dy & 3) * 4 + (dz & 3)
    step = jnp.full(shift.shape, SELF, jnp.int32)
    for number, (x, y, z) in enumerate(ORDER[:SELF]):
        step = jnp.where(shift == x * 16 + y * 4 + z, number, step)
    return step


def in_part(step, part):
    begin, steps, _ = PARTS[part]
    return (step >= begin) & (step < begin + steps)


def chip_places():
    sub, lane = iota((CLUSTERS, CLUSTERS), 0), iota((CLUSTERS, CLUSTERS), 1)
    return onehot((sub == lane) | (sub == (CLUSTERS - 1) - lane))


def excess(totals):
    lane = iota(totals.shape, 1)
    return jnp.where(lane < CHIPS, jnp.maximum(totals - BASE, 0.0), 0.0)


def receive_plan(table, rank, my_x, my_y, my_z):
    chip = my_x * 16 + my_y * 4 + my_z
    heads = table.astype(jnp.int32)
    counts = (heads & 1023).astype(F32)
    differ = jnp.where((heads >> 10).astype(F32) != rank, 1.0, 0.0)
    fault = across(down(differ))
    both = dot(counts.astype(BF16), chip_places())
    over = excess(both)
    lanes = iota((CHIPS, CLUSTERS), 1)
    sender = iota((CHIPS, 1), 0)
    source, target = iota((CHIPS, CHIPS), 0), iota((CHIPS, CHIPS), 1)

    same_line = (source >> 2) == (target >> 2)
    over_total = across(over)
    over_row = as_row(over_total)
    line_start = across(pick(same_line & (target < source), over_row))
    line_total = across(pick(same_line, over_row))
    fault = fault + down(jnp.where(line_total > POOL, 1.0, 0.0))
    start = line_start + across(pick(lanes < chip, over))
    number = across(pick(lanes == chip, over))

    to_chip = iota((1, CLUSTERS), 1)
    route = step_to(
        (to_chip >> 4) - (sender >> 4), ((to_chip >> 2) & 3) - ((sender >> 2) & 3), (to_chip & 3) - (sender & 3)
    )
    based = jnp.where(lanes < CHIPS, jnp.minimum(both, float(BASE)), 0.0)
    for part, (_, _, room) in enumerate(PARTS):
        held = down(pick(in_part(route, part), based))
        if part == LAST:
            held = held + down(over)
        fault = fault + across(jnp.where(held > room, 1.0, 0.0))

    first = across(pick(lanes == chip, counts))
    second = across(pick(lanes == (CLUSTERS - 1) - chip, counts))
    place = (lanes & (POOL - 1)).astype(F32) - start
    mine = ((sender >> 2) == (lanes >> 3)) & (place >= 0.0) & (place < number)
    over_first = down(jnp.where(mine & (place + BASE < first), 1.0, 0.0))
    over_second = down(jnp.where(mine & (place + BASE >= first), 1.0, 0.0))
    over_first_total, over_second_total = across(over_first), across(over_second)
    earlier = onehot(iota((CLUSTERS, CLUSTERS), 0) < iota((CLUSTERS, CLUSTERS), 1))
    sub = iota((16, CLUSTERS), 0)
    before = dot((pick(sub == 0, over_first) + pick(sub == 1, over_second)).astype(BF16), earlier)

    base_first = jnp.minimum(first, float(BASE))
    base_second = jnp.minimum(first + second, float(BASE)) - base_first
    first_row, second_row = as_row(base_first), as_row(base_second)

    def my_step(other):
        return step_to(my_x - (other >> 4), my_y - ((other >> 2) & 3), my_z - (other & 3))

    step_column, step_row = my_step(sender), my_step(iota((1, CHIPS), 1))
    plans = []
    ends = []
    for part, (begin, steps, _) in enumerate(PARTS):
        inside = in_part(step_column, part)
        ahead = (target < source) & in_part(step_row, part)
        first_total = down(pick(inside, base_first))
        second_total = down(pick(inside, base_second))
        last = part == LAST
        first_end = first_total + over_first_total if last else first_total
        first_start = across(pick(ahead, first_row))
        second_start = across(pick(ahead, second_row)) + first_end
        spread = step_column - begin == (iota((CHIPS, steps * BASE), 1) >> 4)
        head, tail, head_start, tail_start = [
            down(pick(spread, column)) for column in (base_first, base_second, first_start, second_start)
        ]
        slot = (iota((1, steps * BASE), 1) & (BASE - 1)).astype(F32)
        later = jnp.where(slot < head + tail, tail_start + (slot - head), -1.0)
        plan = jnp.where(slot < head, head_start + slot, later)
        held_end = first_end + second_total
        if last:
            over_row_of = jnp.where(over_second > 0.5, held_end + before[1:2], -1.0)
            over_row_of = jnp.where(over_first > 0.5, first_total + before[0:1], over_row_of)
            plan = jnp.concatenate([plan[:, : steps * BASE - CLUSTERS], over_row_of], axis=1)
            held_end = held_end + over_second_total
        plans.append(plan)
        ends.append((first_end, held_end))
    return plans, ends, line_start, over_total, fault


def kernel(
    x_hbm, assign_hbm, owner_hbm, count_hbm, index_hbm,
    max_ref, cos_ref, fault_ref,
    x_ref, assign_ref, owner_ref, count_ref, index_ref,
    send, got, heads, own_over, line_over, send_over, got_over, pick_0, pick_1, pick_2,
    mine, theirs, facts, sums, their_sums, back, returned,
    load_sem, send_sem, recv_sem,
):
    grp, blk = lax.axis_index("grp"), lax.axis_index("blk")
    my_x, my_y, my_z, core = grp // 4, grp % 4, blk // 2, blk % 2
    my_chip = grp * 4 + my_z
    picks = (pick_0, pick_1, pick_2)
    along_x = [((my_x + d) % 4) * 4 for d in range(4)]
    along_y = [(my_y + d) % 4 for d in range(4)]
    along_z = [((my_z + d) % 4) * 2 + core for d in range(4)]
    other_core = {"grp": grp, "blk": my_z * 2 + (1 - core)}

    def device_at(step, sign):
        dx, dy, dz = [(sign * d) % 4 for d in ORDER[step]]
        return {"grp": along_x[dx] + along_y[dy], "blk": along_z[dz]}

    def remote(source, target, number, device):
        return pltpu.make_async_remote_copy(
            src_ref=source,
            dst_ref=target,
            send_sem=send_sem.at[number],
            recv_sem=recv_sem.at[number],
            device_id=device,
            device_id_type=pl.DeviceIdType.MESH,
        )

    def await_blocks(ref, number, semaphore):
        block = ref.at[pl.ds(0, number)]
        pltpu.make_async_copy(block, block, semaphore).wait()

    HEAD_Z, HEAD_Y, HEAD_X, LINE, OVER, FACTS, SUMS, BACK, SWAP, PART = 0, 1, 2, 3, 4, 5, 6, 7, 8, 11
    messages = [min(begin + steps, SELF) - begin for begin, steps, _ in PARTS]

    loads = [
        pltpu.make_async_copy(source, target, load_sem.at[number])
        for number, (source, target) in enumerate(
            (
                (assign_hbm, assign_ref),
                (owner_hbm, owner_ref),
                (count_hbm, count_ref),
                (index_hbm, index_ref),
                (x_hbm, x_ref),
            )
        )
    ]
    for load in loads:
        load.start()
    barrier = pltpu.get_barrier_semaphore()
    for device in [device_at(step, 1) for step in range(SELF)] + [other_core]:
        pl.semaphore_signal(barrier, inc=1, device_id=device, device_id_type=pl.DeviceIdType.MESH)
    for load in loads[:-1]:
        load.wait()

    rank, count_column = rank_groups(count_ref)
    group, chip, slot, place_counts = place_documents(assign_ref, owner_ref, rank)
    step_of = step_to((chip >> 4) - my_x, ((chip >> 2) & 3) - my_y, (chip & 3) - my_z)
    in_base = slot < BASE
    send_slot = jnp.where(in_base, step_of * BASE + slot, -1)
    heads[my_chip] = place_counts + 1024.0 * rank
    loads[-1].wait()

    def pack(first, stop):
        slots = iota(((stop - first) * BASE, ROWS), 0) + first * BASE
        rows = dot(onehot(slots == send_slot), x_ref[...]).astype(BF16)
        send[pl.ds(first, stop - first)] = rows.reshape(stop - first, BASE, WIDTH)

    def post(first, stop):
        for step in range(first, min(stop, SELF)):
            number = max(part for part in range(len(PARTS)) if PARTS[part][0] <= step)
            remote(send.at[step], got.at[step], PART + number, device_at(step, 1)).start()

    def share_heads(first, number, semaphore, devices):
        block = heads.at[pl.ds(first, number)]
        for device in devices:
            remote(block, block, semaphore, device).start()

    pack(0, 24)
    pl.semaphore_wait(barrier, CHIPS)
    share_heads(my_chip, 1, HEAD_Z, [{"grp": grp, "blk": along_z[d]} for d in range(1, 4)])
    post(0, 8)
    place_counts_16 = place_counts + jnp.zeros((16, CLUSTERS), F32)
    own_excess = excess(dot(place_counts_16.astype(BF16), chip_places())[0:1])
    eye = iota((CHIPS, CLUSTERS), 0) == iota((CHIPS, CLUSTERS), 1)
    excess_column = across(pick(eye, own_excess))
    over_slot = down(pick(iota((CHIPS, ROWS), 0) < chip, excess_column)).astype(jnp.int32) + (slot - BASE)
    over_slot = jnp.where(in_base, -1, over_slot)
    own_over[...] = dot(onehot(iota((BASE, ROWS), 0) == over_slot), x_ref[...]).astype(BF16)
    line_over[my_z] = own_over[...]
    for d in range(1, DEPTH):
        remote(own_over, line_over.at[my_z], LINE, {"grp": grp, "blk": along_z[d]}).start()
    await_blocks(heads, 3, recv_sem.at[HEAD_Z])
    share_heads(grp * 4, 4, HEAD_Y, [{"grp": along_x[0] + along_y[d], "blk": blk} for d in range(1, 4)])
    post(8, 16)
    pack(24, 48)
    await_blocks(heads, 12, recv_sem.at[HEAD_Y])
    share_heads(my_x * 16, 16, HEAD_X, [{"grp": along_x[d] + along_y[0], "blk": blk} for d in range(1, 4)])
    post(16, 40)
    pack(48, CHIPS)
    got[SELF] = send[SELF]

    await_blocks(heads, 48, recv_sem.at[HEAD_X])
    table = heads[...].reshape(CHIPS, CLUSTERS)
    plans, ends, line_start, over_total, fault = receive_plan(table, rank, my_x, my_y, my_z)

    await_blocks(line_over, DEPTH - 1, recv_sem.at[LINE])
    sender = iota((CHIPS, 1), 0)
    at = sender == grp * 4 + (iota((CHIPS, DEPTH * BASE), 1) >> 4)
    begin = down(pick(at, line_start))
    number = down(pick(at, over_total))
    order = (iota((1, DEPTH * BASE), 1) & (BASE - 1)).astype(F32)
    order = jnp.where(order < number, begin + order, -1.0)
    my_start = down(pick(sender == my_chip, line_start))
    rows = iota((2 * POOL, DEPTH * BASE), 0).astype(F32)
    blocks = line_over[...].reshape(DEPTH * BASE, WIDTH)
    left = dot(onehot((rows == order) & (rows < POOL)), blocks[:, :HALF])
    right = dot(onehot((rows - POOL == order) & (rows >= POOL)), blocks[:, HALF:])
    send_over[...] = (left + right).astype(BF16)
    got_over[grp] = send_over[...]
    for step in range(1, LINES):
        low, middle = step % 4, step // 4
        device = {"grp": along_x[low] + along_y[(middle + low) % 4], "blk": blk}
        remote(send_over, got_over.at[grp], OVER, device).start()
    post(40, CHIPS)

    missing = missing_documents(index_ref, count_column, group)
    row = iota((8, 128), 0)
    told = pick(row == 6, rank) + pick(row == 7, jnp.where(iota((1, 128), 1) == 0, fault, missing))
    for part, (first_end, held_end) in enumerate(ends):
        told = told + pick(row == part, first_end) + pick(row == 3 + part, held_end)
        picks[part][...] = onehot(iota(picks[part].shape, 0).astype(F32) == plans[part])
    facts[0] = told
    swap_facts = remote(facts.at[0], facts.at[1], FACTS, other_core)
    swap_facts.start()

    best = [jnp.full((1, room), -1.0, F32) for _, _, room in PARTS]
    their_ends = []
    totals = [jnp.zeros((1, WIDTH), F32), jnp.zeros((1, WIDTH), F32)]
    swaps = []

    def window(part):
        return pl.ds(STARTS[part], PARTS[part][2])

    def compare(keys, key_part, query_part, key_ends, itself):
        scores = dot_rows(keys[window(key_part)], mine[window(query_part)])
        first, held = key_ends[key_part]
        key_number = iota((PARTS[key_part][2], 1), 0).astype(F32)
        query_number = iota((1, PARTS[query_part][2]), 1).astype(F32)
        kind = jnp.where(key_number < first, 0.0, jnp.where(key_number < held, 1.0, 2.0))
        matched = kind == jnp.where(query_number < ends[query_part][0], 0.0, 1.0)
        if itself and key_part == query_part:
            matched = matched & (key_number != query_number)
        scores = jnp.max(jnp.where(matched, scores, -1.0), axis=0, keepdims=True)
        best[query_part] = jnp.maximum(best[query_part], scores)

    for part, (begin, steps, room) in enumerate(PARTS):
        if part == LAST:
            await_blocks(got_over, LINES - 1, recv_sem.at[OVER])
            halves = got_over[...].reshape(LINES * 2 * POOL, HALF)
            shape = (LINES * POOL, LINES * 2 * POOL)
            to, at = iota(shape, 0), iota(shape, 1)
            same = ((to >> 3) == (at >> 4)) & ((to & 7) == (at & 7))
            left = dot(onehot(same & ((at & POOL) == 0)), halves)
            right = dot(onehot(same & ((at & POOL) != 0)), halves)
            whole = jnp.concatenate([left, right], axis=1).astype(BF16)
            got[pl.ds(CHIPS, TOTAL - CHIPS)] = whole.reshape(TOTAL - CHIPS, BASE, WIDTH)
        await_blocks(got, messages[part], recv_sem.at[PART + part])
        rows = dot(picks[part][...], got[pl.ds(begin, steps)].reshape(steps * BASE, WIDTH))
        unit = rows * lax.rsqrt(across(rows * rows) + EPSILON)
        mine[window(part)] = unit.astype(BF16)
        swap = remote(mine.at[window(part)], theirs.at[window(part)], SWAP + part, other_core)
        swap.start()
        swaps.append(swap)
        is_first = iota((room, 1), 0).astype(F32) < ends[part][0]
        totals[0] = totals[0] + down(pick(is_first, unit))
        totals[1] = totals[1] + down(jnp.where(is_first, 0.0, unit))
        if part == LAST:
            row = iota((8, WIDTH), 0)
            sums[...] = pick(row == 0, totals[0]) + pick(row == 1, totals[1])
            swap_sums = remote(sums, their_sums, SUMS, other_core)
            swap_sums.start()
        for other in range(part + 1):
            compare(mine, part, other, ends, True)
            if other != part:
                compare(mine, other, part, ends, True)
        if part == 0:
            swap_facts.wait()
            their_told = facts[1]
            for number in range(len(PARTS)):
                their_ends.append((their_told[number : number + 1, 0:1], their_told[3 + number : 4 + number, 0:1]))
        else:
            for other in range(part - 1):
                compare(theirs, other, part, their_ends, False)
            swaps[part - 1].wait()
            for other in range(part + 1):
                compare(theirs, part - 1, other, their_ends, False)

    swap_sums.wait()
    total = sums[...] + their_sums[...]
    centre = total * lax.rsqrt(across(total * total) + EPSILON)
    near = dot_rows(jnp.concatenate(thirds(centre), axis=0).astype(BF16), mine[...])
    near = near[0:8] + near[8:16] + near[16:24]
    swaps[LAST].wait()
    for other in range(len(PARTS)):
        compare(theirs, LAST, other, their_ends, False)

    poison = missing + their_told[7:8, 1:2] > 0.5
    tiles = CHIPS * BASE // 128
    for part, (begin, steps, room) in enumerate(PARTS):
        row = iota((8, room), 0)
        query_number = iota((1, room), 1).astype(F32)
        some = near[:, STARTS[part] : STARTS[part] + room]
        some = jnp.where(query_number < ends[part][0], some[0:1], some[1:2])
        values = jnp.zeros((8, room), F32)
        for number, term in enumerate(thirds(best[part]) + thirds(some)):
            values = jnp.where(row == number, term, values)
        out = dot(values.astype(BF16), picks[part][...])
        for kind in range(2):
            line = out[3 * kind : 3 * kind + 1] + out[3 * kind + 1 : 3 * kind + 2] + out[3 * kind + 2 : 3 * kind + 3]
            line = jnp.where(poison, NONE, line)
            for tile in range(steps * BASE // 128):
                piece = line[:, tile * 128 : (tile + 1) * 128]
                to = begin * BASE // 128 + tile
                if to < tiles:
                    back[to, kind : kind + 1, :] = piece
                else:
                    for each in range(tiles):
                        back[each, 2 + kind : 3 + kind, :] = piece
    returned[SELF] = back[SELF // 8]
    for step in range(SELF):
        remote(back.at[step // 8], returned.at[step], BACK, device_at(step, -1)).start()

    differ = across(jnp.where(their_told[6:7] != rank, 1.0, 0.0))
    fault = fault + their_told[7:8, 0:1] + differ
    chosen = onehot(iota((CHIPS, ROWS), 0) == step_of)
    sub = iota((128, ROWS), 0)
    at_base = (sub == (step_of & 7) * BASE + slot) & in_base
    at_over = (sub == grp * POOL + my_start.astype(jnp.int32) + over_slot) & (~in_base)

    await_blocks(returned, CHIPS - 1, recv_sem.at[BACK])
    found = []
    for number in range(4):
        line = returned[:, number, :]
        if number == 0:
            poisoned = across(down(jnp.where(line > 0.5 * NONE, 1.0, 0.0)))
            fault_ref[...] = jnp.where(fault + poisoned > 0.5, 1, 0) + jnp.zeros((1, 128), jnp.int32)
        terms = jnp.concatenate(thirds(line), axis=1).astype(BF16)
        out = lax.dot_general(terms, chosen, (((0,), (0,)), ((), ())), preferred_element_type=F32)
        found.append(out[0:128] + out[128:256] + out[256:384])
    max_ref[...] = down(pick(at_base, found[0]) + pick(at_over, found[2]))
    cos_ref[...] = down(pick(at_base, found[1]) + pick(at_over, found[3]))

    await_blocks(heads, 3, send_sem.at[HEAD_Z])
    await_blocks(heads, 12, send_sem.at[HEAD_Y])
    await_blocks(heads, 48, send_sem.at[HEAD_X])
    await_blocks(line_over, DEPTH - 1, send_sem.at[LINE])
    await_blocks(got_over, LINES - 1, send_sem.at[OVER])
    await_blocks(returned, CHIPS - 1, send_sem.at[BACK])
    for part in range(len(PARTS)):
        await_blocks(got, messages[part], send_sem.at[PART + part])


def routed(embeddings, assign, owner, send_count, send_index):
    return pl.pallas_call(
        kernel,
        out_shape=(
            jax.ShapeDtypeStruct((1, ROWS), F32),
            jax.ShapeDtypeStruct((1, ROWS), F32),
            jax.ShapeDtypeStruct((1, 128), jnp.int32),
        ),
        in_specs=[pl.BlockSpec(memory_space=pl.ANY)] * 5,
        out_specs=(pl.BlockSpec(memory_space=pltpu.VMEM),) * 3,
        scratch_shapes=[
            pltpu.VMEM((ROWS, WIDTH), BF16),
            pltpu.VMEM((1, ROWS), jnp.int32),
            pltpu.VMEM((1, CLUSTERS), jnp.int32),
            pltpu.VMEM((1, GROUPS), jnp.int32),
            pltpu.VMEM((GROUPS, CAP), jnp.int32),
            pltpu.VMEM((CHIPS, BASE, WIDTH), BF16),
            pltpu.VMEM((TOTAL, BASE, WIDTH), BF16),
            pltpu.VMEM((CHIPS, 1, 128), F32),
            pltpu.VMEM((BASE, WIDTH), BF16),
            pltpu.VMEM((DEPTH, BASE, WIDTH), BF16),
            pltpu.VMEM((2 * POOL, HALF), BF16),
            pltpu.VMEM((LINES, 2 * POOL, HALF), BF16),
            *[pltpu.VMEM((room, steps * BASE), BF16) for _, steps, room in PARTS],
            pltpu.VMEM((HELD, WIDTH), BF16),
            pltpu.VMEM((HELD, WIDTH), BF16),
            pltpu.VMEM((2, 8, 128), F32),
            pltpu.VMEM((8, WIDTH), F32),
            pltpu.VMEM((8, WIDTH), F32),
            pltpu.VMEM((CHIPS * BASE // 128, 4, 128), F32),
            pltpu.VMEM((CHIPS, 4, 128), F32),
            pltpu.SemaphoreType.DMA((5,)),
            pltpu.SemaphoreType.DMA((14,)),
            pltpu.SemaphoreType.DMA((14,)),
        ],
        compiler_params=pltpu.CompilerParams(
            collective_id=0, has_side_effects=True, vmem_limit_bytes=48 * 1024 * 1024
        ),
    )(
        embeddings,
        assign.reshape(1, ROWS),
        owner.reshape(1, CLUSTERS),
        send_count,
        send_index[0],
    )


def body(embeddings, assign, owner, send_count, send_index):
    arguments = (embeddings, assign, owner, send_count, send_index)
    max_sim, centroid_cos, fault = routed(*arguments)
    return lax.cond(
        fault[0, 0] != 0,
        lambda: general(*arguments),
        lambda: (max_sim.reshape(ROWS), centroid_cos.reshape(ROWS)),
    )


def solution(mesh):
    placed = (
        P(("grp", "blk"), None),
        P(("grp", "blk")),
        P(),
        P(("grp", "blk"), None),
        P(("grp", "blk"), None, None),
    )
    return jax.shard_map(
        body,
        mesh=mesh,
        in_specs=placed,
        out_specs=(P(("grp", "blk")), P(("grp", "blk"))),
        check_vma=False,
    )
```

profile of v0, /device:TPU:1, one launch (start us, length us, event | category | flops | bytes accessed | tf_op | source)
XLA Modules:
  0.0 63.0 jit_solution(9262508602357992218)
XLA Ops:
  7.2 47.5 %shard_map.72 = (f32[1,512]{1,0:T(1,128)S(1)}, f32[1,512]{1,0:T(1,128)S(1)}, s32[1,128]{1,0:T(1,128)S(1)}) custom-call(bf16[512,768]{1,0:T(8,128)(2,1)} %x_hbm.1, s32[1,512]{1,0:T(1,128)} %bitcast.49, s32[1,128]{1,0:T(1,128)} %bitcast.48, s32[1,16]{1,0:T(1,128)} %count_hbm.1, s32[16,64]{1,0:T(8,128)} %bitcast.53), custom_call_target="tpu_custom_call" | custom-call | tf_op jit(solution)/shard_map/pallas_call | solution.py:589
  54.7 0.2 conditional.1
  55.0 0.6 copy.24
  55.5 0.6 copy.25
where the time goes:
time: 63.1 us; the launch traced here: 63 us
  Pallas kernels  47.5 us (75%)
  between operations  14.1 us (22%)
  local copies, waits for them, and re-layouts  1.16 us (2%)
    pallas_call x1, Pallas kernels, routed(): pl.pallas_call(kernel, out_shape=(jax.ShapeDtypeStruct((1, ROWS), F32), j...  47.5 us

commit v1 on v0

--- a/solution.py
+++ b/solution.py
@@ -202,25 +202,39 @@
     return across(jnp.where(down(hits) > 0.5, 0.0, 1.0))
 
 
-def send_order():
-    order = []
-    for step in range(CHIPS):
-        high, middle, low = step // 16, (step // 4) % 4, step % 4
-        order.append((low, (middle + low) % 4, (high + middle + low) % 4))
-    near = [shift for shift in order if sum(min(d, 4 - d) for d in shift) <= 1] + [(2, 0, 0)]
-    near.sort(key=lambda shift: -sum(min(d, 4 - d) for d in shift))
-    return [shift for shift in order if shift not in near] + near
-
-
-ORDER = send_order()
+ORDERS = (
+    (
+        (2, 2, 0), (3, 3, 1), (3, 3, 3), (0, 2, 0), (3, 1, 1), (1, 1, 1), (1, 3, 3), (0, 2, 2), (0, 0, 2),
+        (1, 1, 3), (1, 3, 1), (3, 1, 3), (0, 2, 3), (1, 1, 2), (0, 2, 1), (1, 3, 2), (2, 0, 3), (3, 1, 2),
+        (2, 0, 1), (3, 3, 2), (1, 0, 1), (0, 3, 2), (1, 2, 3), (2, 3, 0), (3, 0, 1), (2, 1, 0), (1, 2, 1),
+        (0, 1, 2), (1, 0, 3), (3, 1, 0), (0, 1, 3), (1, 2, 0), (0, 1, 1), (1, 0, 2), (0, 3, 3), (3, 0, 2),
+        (2, 3, 3), (3, 2, 0), (2, 1, 3), (3, 2, 3), (0, 3, 1), (3, 3, 0), (2, 1, 1), (1, 1, 0), (3, 2, 1),
+        (1, 3, 0), (2, 3, 1), (3, 0, 3), (2, 1, 2), (3, 2, 2), (2, 2, 2), (2, 3, 2), (2, 2, 3), (1, 2, 2),
+        (2, 2, 1), (2, 0, 2), (2, 0, 0), (0, 0, 3), (0, 0, 1), (0, 3, 0), (3, 0, 0), (1, 0, 0), (0, 1, 0),
+    ),
+    (
+        (0, 0, 2), (1, 1, 3), (1, 1, 1), (2, 0, 2), (1, 3, 3), (3, 3, 3), (3, 1, 1), (2, 0, 0), (2, 2, 0),
+        (3, 3, 1), (3, 1, 3), (1, 3, 1), (2, 0, 1), (3, 3, 0), (2, 0, 3), (3, 1, 0), (0, 2, 1), (1, 3, 0),
+        (0, 2, 3), (1, 1, 0), (3, 2, 3), (2, 1, 0), (3, 0, 1), (0, 1, 2), (1, 2, 3), (0, 3, 2), (3, 0, 3),
+        (2, 3, 0), (3, 2, 1), (1, 3, 2), (2, 3, 1), (3, 0, 2), (2, 3, 3), (3, 2, 0), (2, 1, 1), (1, 2, 0),
+        (0, 1, 1), (1, 0, 2), (0, 3, 1), (1, 0, 1), (2, 1, 3), (1, 1, 2), (0, 3, 3), (3, 3, 2), (1, 0, 3),
+        (3, 1, 2), (0, 1, 3), (1, 2, 1), (2, 2, 1), (2, 2, 2), (2, 2, 3), (1, 2, 2), (3, 2, 2), (2, 3, 2),
+        (0, 2, 2), (2, 1, 2), (0, 2, 0), (3, 0, 0), (0, 1, 0), (1, 0, 0), (0, 0, 3), (0, 0, 1), (0, 3, 0),
+    ),
+)
 SELF = CHIPS - 1
 
 
-def step_to(dx, dy, dz):
+def by_core(first, second, core):
+    return first + core * (second - first) if first != second else first
+
+
+def step_to(dx, dy, dz, core):
     shift = (dx & 3) * 16 + (dy & 3) * 4 + (dz & 3)
     step = jnp.full(shift.shape, SELF, jnp.int32)
-    for number, (x, y, z) in enumerate(ORDER[:SELF]):
-        step = jnp.where(shift == x * 16 + y * 4 + z, number, step)
+    for number in range(SELF):
+        codes = [x * 16 + y * 4 + z for x, y, z in (order[number] for order in ORDERS)]
+        step = jnp.where(shift == by_core(*codes, core), number, step)
     return step
 
 
@@ -239,7 +253,7 @@
     return jnp.where(lane < CHIPS, jnp.maximum(totals - BASE, 0.0), 0.0)
 
 
-def receive_plan(table, rank, my_x, my_y, my_z):
+def receive_plan(table, rank, my_x, my_y, my_z, core):
     chip = my_x * 16 + my_y * 4 + my_z
     heads = table.astype(jnp.int32)
     counts = (heads & 1023).astype(F32)
@@ -262,7 +276,7 @@
 
     to_chip = iota((1, CLUSTERS), 1)
     route = step_to(
-        (to_chip >> 4) - (sender >> 4), ((to_chip >> 2) & 3) - ((sender >> 2) & 3), (to_chip & 3) - (sender & 3)
+        (to_chip >> 4) - (sender >> 4), ((to_chip >> 2) & 3) - ((sender >> 2) & 3), (to_chip & 3) - (sender & 3), core
     )
     based = jnp.where(lanes < CHIPS, jnp.minimum(both, float(BASE)), 0.0)
     for part, (_, _, room) in enumerate(PARTS):
@@ -287,7 +301,7 @@
     first_row, second_row = as_row(base_first), as_row(base_second)
 
     def my_step(other):
-        return step_to(my_x - (other >> 4), my_y - ((other >> 2) & 3), my_z - (other & 3))
+        return step_to(my_x - (other >> 4), my_y - ((other >> 2) & 3), my_z - (other & 3), core)
 
     step_column, step_row = my_step(sender), my_step(iota((1, CHIPS), 1))
     plans = []
@@ -321,7 +335,7 @@
 
 def kernel(
     x_hbm, assign_hbm, owner_hbm, count_hbm, index_hbm,
-    max_ref, cos_ref, fault_ref,
+    out_ref, fault_ref,
     x_ref, assign_ref, owner_ref, count_ref, index_ref,
     send, got, heads, own_over, line_over, send_over, got_over, pick_0, pick_1, pick_2,
     mine, theirs, facts, sums, their_sums, back, returned,
@@ -337,8 +351,9 @@
     other_core = {"grp": grp, "blk": my_z * 2 + (1 - core)}
 
     def device_at(step, sign):
-        dx, dy, dz = [(sign * d) % 4 for d in ORDER[step]]
-        return {"grp": along_x[dx] + along_y[dy], "blk": along_z[dz]}
+        shifts = [[(sign * d) % 4 for d in order[step]] for order in ORDERS]
+        x, y, z = [(my + by_core(d0, d1, core)) % 4 for my, d0, d1 in zip((my_x, my_y, my_z), *shifts)]
+        return {"grp": x * 4 + y, "blk": z * 2 + core}
 
     def remote(source, target, number, device):
         return pltpu.make_async_remote_copy(
@@ -379,7 +394,7 @@
 
     rank, count_column = rank_groups(count_ref)
     group, chip, slot, place_counts = place_documents(assign_ref, owner_ref, rank)
-    step_of = step_to((chip >> 4) - my_x, ((chip >> 2) & 3) - my_y, (chip & 3) - my_z)
+    step_of = step_to((chip >> 4) - my_x, ((chip >> 2) & 3) - my_y, (chip & 3) - my_z, core)
     in_base = slot < BASE
     send_slot = jnp.where(in_base, step_of * BASE + slot, -1)
     heads[my_chip] = place_counts + 1024.0 * rank
@@ -426,7 +441,7 @@
 
     await_blocks(heads, 48, recv_sem.at[HEAD_X])
     table = heads[...].reshape(CHIPS, CLUSTERS)
-    plans, ends, line_start, over_total, fault = receive_plan(table, rank, my_x, my_y, my_z)
+    plans, ends, line_start, over_total, fault = receive_plan(table, rank, my_x, my_y, my_z, core)
 
     await_blocks(line_over, DEPTH - 1, recv_sem.at[LINE])
     sender = iota((CHIPS, 1), 0)
@@ -572,8 +587,8 @@
         terms = jnp.concatenate(thirds(line), axis=1).astype(BF16)
         out = lax.dot_general(terms, chosen, (((0,), (0,)), ((), ())), preferred_element_type=F32)
         found.append(out[0:128] + out[128:256] + out[256:384])
-    max_ref[...] = down(pick(at_base, found[0]) + pick(at_over, found[2]))
-    cos_ref[...] = down(pick(at_base, found[1]) + pick(at_over, found[3]))
+    out_ref[0:1] = down(pick(at_base, found[0]) + pick(at_over, found[2]))
+    out_ref[1:2] = down(pick(at_base, found[1]) + pick(at_over, found[3]))
 
     await_blocks(heads, 3, send_sem.at[HEAD_Z])
     await_blocks(heads, 12, send_sem.at[HEAD_Y])
@@ -589,12 +604,11 @@
     return pl.pallas_call(
         kernel,
         out_shape=(
-            jax.ShapeDtypeStruct((1, ROWS), F32),
-            jax.ShapeDtypeStruct((1, ROWS), F32),
+            jax.ShapeDtypeStruct((2, ROWS), F32),
             jax.ShapeDtypeStruct((1, 128), jnp.int32),
         ),
         in_specs=[pl.BlockSpec(memory_space=pl.ANY)] * 5,
-        out_specs=(pl.BlockSpec(memory_space=pltpu.VMEM),) * 3,
+        out_specs=(pl.BlockSpec(memory_space=pltpu.VMEM),) * 2,
         scratch_shapes=[
             pltpu.VMEM((ROWS, WIDTH), BF16),
             pltpu.VMEM((1, ROWS), jnp.int32),
@@ -634,12 +648,9 @@
 
 def body(embeddings, assign, owner, send_count, send_index):
     arguments = (embeddings, assign, owner, send_count, send_index)
-    max_sim, centroid_cos, fault = routed(*arguments)
-    return lax.cond(
-        fault[0, 0] != 0,
-        lambda: general(*arguments),
-        lambda: (max_sim.reshape(ROWS), centroid_cos.reshape(ROWS)),
-    )
+    results, fault = routed(*arguments)
+    results = lax.cond(fault[0, 0] != 0, lambda: jnp.stack(general(*arguments)), lambda: results)
+    return results[0], results[1]
 
 
 def solution(mesh):

time: 63.1 us -> 63 us (level)
    unnamed x2 -> x0, local copies, waits for them, and re-layouts: 1.16 us -> none
where the time goes in v1:
time: 63 us; the launch traced here: 62.9 us
  Pallas kernels  48 us (76%)
  between operations  14.1 us (22%)
    pallas_call x1, Pallas kernels, routed(): pl.pallas_call(kernel, out_shape=(jax.ShapeDtypeStruct((2, ROWS), F32), j...  48 us

profile of v1, /device:TPU:1, one launch (start us, length us, event | category | flops | bytes accessed | tf_op | source)
XLA Modules:
  0.0 62.9 jit_solution(4875228124308780762)
XLA Ops:
  7.2 48.0 %shard_map.68 = (f32[2,512]{1,0:T(2,128)S(1)}, s32[1,128]{1,0:T(1,128)S(1)}) custom-call(bf16[512,768]{1,0:T(8,128)(2,1)} %x_hbm.1, s32[1,512]{1,0:T(1,128)} %bitcast.51, s32[1,128]{1,0:T(1,128)} %bitcast.50, s32[1,16]{1,0:T(1,128)} %count_hbm.1, s32[16,64]{1,0:T(8,128)} %bitcast.55), custom_call_target="tpu_custom_call" | custom-call | tf_op jit(solution)/shard_map/pallas_call | solution.py:604
  55.2 0.2 conditional.1
  55.5 0.6 fusion.16
